TPU v7x, 32 devices: a whole 2x2x4 slice. The times are simulated.
32 devices in a mesh: ctx: 4 (over y, x), ep: 8 (over z, core).
Axes of the slice: x: 2, y: 2, z: 4, core: 2. Of those that a mesh axis runs over, the one named last changes fastest.
Arguments:
- latent_cache: bfloat16 [2048, 576], P(('ctx', 'ep'))
- prefill_query: bfloat16 [256, 32, 576], P('ctx', 'ep')
- prompt_lengths: int32 [2], replicated, may hold values from 1 to 1536, 2048 in all
- group_of: int32 [4], replicated, may hold values from 0 to 1, as said below
- decode_latent: bfloat16 [4, 2, 64, 576], P('ctx')
- decode_query: bfloat16 [4, 2, 64, 32, 576], P('ctx', None, None, 'ep')
Outputs:
- prefill_out: bfloat16 [256, 32, 512], P('ctx', 'ep')
- decode_out: bfloat16 [4, 2, 64, 32, 512], P('ctx', None, None, 'ep')
Inputs may be any that keep to these rules, and one draw needn't show every extreme that they name: `prompt_lengths`: the 2 prompt lengths add up to 2048, and the longest is at most 1536. `group_of`: every prompt is decoded by exactly 2 groups.
All inputs are finite; a program needn't handle non-finite values.
Results may differ from a plain program's by a relative error of at most 0.004.
Values may be sent and summed in bfloat16 or wider, within the bound.
A program may use at most 128 MiB of HBM per device.

v0:
```python
import jax
import jax.numpy as jnp
from jax import lax
from jax.sharding import PartitionSpec as P

LAT = 512


SCALE = 192 ** (-0.5)
FLOOR = -1e30


def request_segment(positions, ends):
    return jnp.sum((positions[:, None] >= ends[None, :]).astype(jnp.int32), axis=1)


def decode_group(prefix, live, new_rows, queries):
    steps, count, heads, width = queries.shape
    reach = prefix.shape[0]
    results = []
    for step in range(steps):
        query = queries[step]
        flat = query.reshape(count * heads, width)
        prefix_scores = (
            lax.dot_general(
                flat, prefix, (((1,), (1,)), ((), ())), preferred_element_type=jnp.float32
            )
            * SCALE
        )
        prefix_scores = jnp.where(live[None, :], prefix_scores, FLOOR).reshape(count, heads, reach)
        own = new_rows[: step + 1]
        own_scores = (
            jnp.einsum("rhc,src->rhs", query, own, preferred_element_type=jnp.float32) * SCALE
        )
        top = jnp.maximum(jnp.max(prefix_scores, axis=2), jnp.max(own_scores, axis=2))
        prefix_weights = jnp.where(
            live[None, None, :], jnp.exp(prefix_scores - top[:, :, None]), 0.0
        )
        own_weights = jnp.exp(own_scores - top[:, :, None])
        total = jnp.sum(prefix_weights, axis=2) + jnp.sum(own_weights, axis=2)
        mixed = jnp.dot(
            prefix_weights.astype(jnp.bfloat16).reshape(count * heads, reach),
            prefix[:, :LAT],
            preferred_element_type=jnp.float32,
        ).reshape(count, heads, LAT)
        mixed = mixed + jnp.einsum(
            "rhs,src->rhc",
            own_weights.astype(jnp.bfloat16),
            own[:, :, :LAT],
            preferred_element_type=jnp.float32,
        )
        results.append((mixed / total[:, :, None]).astype(jnp.bfloat16))
    return jnp.stack(results)


def body(latent_cache, prefill_query, prompt_lengths, group_of, decode_latent, decode_query):
    block = lax.all_gather(latent_cache, "ep", axis=0, tiled=True)
    rows, width = block.shape
    query_rows = prefill_query.shape[0]
    heads = prefill_query.shape[1]
    ctx_index = lax.axis_index("ctx")
    ctx_count = lax.axis_size("ctx")
    total_rows = rows * ctx_count
    reach = 3 * total_rows // 4
    request_count = prompt_lengths.shape[0]
    span_rows = query_rows * ctx_count // request_count
    ends = jnp.cumsum(prompt_lengths)
    starts = ends - prompt_lengths
    request_ids = jnp.arange(request_count, dtype=jnp.int32)
    query_ids = ctx_index * query_rows + jnp.arange(query_rows, dtype=jnp.int32)
    query_req = query_ids // span_rows
    query_end = jnp.sum(
        jnp.where(query_req[:, None] == request_ids[None, :], ends[None, :], 0), axis=1
    )
    query_pos = jnp.repeat(query_end - span_rows + query_ids % span_rows, heads)
    query_seg = jnp.repeat(query_req, heads)
    flat_query = prefill_query.reshape(query_rows * heads, width)
    piece = lax.all_gather(block, "ctx", axis=0, tiled=True)
    top = jnp.full((query_rows * heads,), FLOOR, jnp.float32)
    count = piece.shape[0]
    key_pos = jnp.arange(count, dtype=jnp.int32)
    key_seg = request_segment(key_pos, ends)
    allowed = (query_seg[:, None] == key_seg[None, :]) & (key_pos[None, :] <= query_pos[:, None])
    scores = (
        lax.dot_general(
            flat_query, piece, (((1,), (1,)), ((), ())), preferred_element_type=jnp.float32
        )
        * SCALE
    )
    scores = jnp.where(allowed, scores, FLOOR)
    new_top = jnp.maximum(top, jnp.max(scores, axis=1))
    weights = jnp.where(allowed, jnp.exp(scores - new_top[:, None]), 0.0)
    total = jnp.sum(weights, axis=1)
    acc = jnp.dot(weights.astype(jnp.bfloat16), piece[:, :LAT], preferred_element_type=jnp.float32)
    top, total, acc = (new_top, total, acc)
    whole = lax.all_gather(block, "ctx", axis=0, tiled=True)
    buffer = jnp.concatenate([whole, jnp.zeros((reach, width), jnp.bfloat16)], axis=0)
    prefill_out = (acc / total[:, None]).astype(jnp.bfloat16).reshape(query_rows, heads, LAT)
    group_ids = jnp.arange(group_of.shape[0], dtype=jnp.int32)
    chosen = jnp.sum(jnp.where(group_ids == ctx_index, group_of, 0))
    owner = request_ids == chosen
    group_start = jnp.sum(jnp.where(owner, starts, 0))
    group_length = jnp.sum(jnp.where(owner, prompt_lengths, 0))
    prefix = lax.dynamic_slice_in_dim(buffer, group_start, reach, 0)
    live = jnp.arange(reach, dtype=jnp.int32) < group_length
    decode_out = decode_group(prefix, live, decode_latent[0], decode_query[0])[None]
    return (prefill_out, decode_out)


def solution(mesh):
    in_specs = (
        P(("ctx", "ep"), None),
        P("ctx", "ep", None),
        P(),
        P(),
        P("ctx", None, None, None),
        P("ctx", None, None, "ep", None),
    )
    out_specs = (P("ctx", "ep", None), P("ctx", None, None, "ep", None))
    return jax.shard_map(body, mesh=mesh, in_specs=in_specs, out_specs=out_specs, check_vma=False)
```

profile of v0, /device:TPU:0, one launch (start us, length us, event | category | flops | bytes accessed | tf_op | source)
XLA Modules:
  0.0 91.2 jit_solution(15226261612377856317)
XLA Ops:
  7.2 0.0 copy-start
  7.2 0.0 all-gather.2.cloned.1.call-start
  7.2 18.2 %all_gather.7 = bf16[512,576]{1,0:T(8,128)(2,1)} all-gather(bf16[64,576]{1,0:T(8,128)(2,1)} %param.6), channel_id=1, replica_groups=mesh['ctx'=4,'ep'=8] {'ep'}, dimensions={0}, use_global_device_ids=true | all-gather | bytes 663552 | tf_op jit(solution)/shard_map/all_gather | solution.py:57
  25.5 0.0 all-gather.2.cloned.1.call-update
  25.5 0.8 reduce-window.8
  26.3 1.3 %fusion.58 = s32[]{:T(128)} fusion(s32[4]{0:T(128)} %param.9, s32[]{:T(128)S(6)} %axis_index.15), kind=kLoop, calls=%fused_computation.78 | loop fusion | flops 11 | bytes 24 | tf_op jit(solution)/shard_map/reduce_sum | solution.py:100
  27.6 1.9 %fusion.56 = (s32[]{:T(128)}, s32[]{:T(128)}) fusion(s32[2]{0:T(128)} %param.8, s32[]{:T(128)} %fusion.58, s32[2,1]{0,1:T(1,128)S(1)} %reduce-window.8), kind=kLoop, calls=%fused_computation.76 | loop fusion | flops 10 | bytes 28 | tf_op jit(solution)/shard_map/reduce_sum | solution.py:103
  30.7 1.3 %fusion.70 = (bf16[1,1,64,4,576]{4,3,2,1,0:T(4,128)(2,1)S(1)}, bf16[1,1,64,4,576]{4,3,2,1,0:T(4,128)(2,1)S(1)}) fusion(bf16[1,2,64,4,576]{4,3,2,1,0:T(4,128)(2,1)} %param.11), kind=kLoop, calls=%fused_computation.92 | loop fusion | bytes 1179648 | tf_op jit(solution)/shard_map/slice | solution.py:22
  32.0 0.0 copy-start.2
  32.0 0.2 reshape_squeeze.6
  32.2 0.2 reshape_squeeze.7
  32.3 0.2 copy.42
  32.5 0.5 fusion.74
  33.1 0.1 reduce_max.51
  33.2 0.1 fusion.54
  33.3 0.1 broadcast_in_dim.95
  33.4 0.1 le.16
  33.5 0.1 broadcast_in_dim.92
  33.6 0.1 eq.42
  33.7 0.9 reshape.142
  35.1 0.7 iota_compare_fusion.1
  35.8 0.1 fusion.52
  35.9 0.7 fusion.47
  36.6 0.5 fusion.42
  37.0 29.2 %all-gather.2.cloned.1.call-done = bf16[2048,576]{1,0:T(8,128)(2,1)} async-done(((bf16[512,576]{1,0:T(8,128)(2,1)}), bf16[2048,576]{1,0:T(8,128)(2,1)}) %all-gather.2.cloned.1.call-update) | async-done | bytes 2359312 | tf_op jit(solution)/shard_map/all_gather | solution.py:78
  66.3 2.4 %fusion.72 = (f32[256]{0:T(256)S(1)}, f32[1536,256]{0,1:T(8,128)S(1)}) fusion(bf16[256,576]{1,0:T(8,128)(2,1)S(1)} %reshape_squeeze.6, s32[]{:T(128)S(6)} %select_n.69, bf16[2048,576]{1,0:T(8,128)(2,1)} %all-gather.2.cloned.1.call-done, pred[1536]{0:T(1024)(128)(4,1)S(1)} %iota_compare_fusion.1), kind=kOutput, calls=%fused_computation.94 | convolution fusion | flops 454164224 | bytes 4229636 | tf_op jit(solution)/shard_map/dot_general | solution.py:25
  68.7 0.1 reduce_max.48
  68.9 0.1 sub.62
  69.0 3.5 %fusion.73 = (f32[256]{0:T(256)S(1)}, f32[1536,256]{0,1:T(8,128)}) fusion(bf16[256,576]{1,0:T(8,128)(2,1)S(1)} %reshape_squeeze.7, s32[]{:T(128)S(6)} %select_n.69, bf16[2048,576]{1,0:T(8,128)(2,1)} %all-gather.2.cloned.1.call-done, pred[1536]{0:T(1024)(128)(4,1)S(1)} %iota_compare_fusion.1), kind=kOutput, calls=%fused_computation.95 | convolution fusion | flops 454164224 | bytes 4229636 | tf_op jit(solution)/shard_map/dot_general | solution.py:25
  72.5 0.1 reduce_max.52
  72.6 2.1 %fusion.9 = (f32[256]{0:T(256)S(1)}, f32[256]{0:T(256)S(1)}, bf16[256,1536]{1,0:T(8,128)(2,1)S(1)}, bf16[256,1536]{1,0:T(8,128)(2,1)S(1)}) fusion(f32[1536,256]{0,1:T(8,128)S(1)} %get-tuple-element.23, f32[256]{0:T(256)S(1)} %sub.62, pred[1536]{0:T(1024)(128)(4,1)S(1)} %iota_compare_fusion.1, f32[1536,256]{0,1:T(8,128)} %get-tuple-element.25, f32[256]{0:T(256)S(1)} %max.16), kind=kLoop, calls=%fused_computation.18 | loop fusion | flops 3145216 | bytes 4724224 | tf_op jit(solution)/shard_map/reduce_sum | solution.py:40
  74.7 0.1 reduce_sum.96
  74.9 0.1 copy.22
  74.9 0.1 copy.23
  75.0 0.2 dot_general.42
  75.2 0.1 reduce_sum.98
  75.3 0.1 fusion.48
  75.5 0.1 copy.27
  75.5 0.2 dot_general.49
  75.7 0.3 fusion.45
  76.1 2.1 %fusion.19 = bf16[1,64,4,512]{3,1,2,0:T(8,128)(2,1)S(1)} fusion(s32[]{:T(128)S(6)} %select_n.69, bf16[2048,576]{1,0:T(8,128)(2,1)} %all-gather.2.cloned.1.call-done, bf16[64,4,1536]{2,1,0:T(4,128)(2,1)S(1)} %dot_general.49, f32[64,4,512]{2,1,0:T(4,128)S(1)} %fusion.45, f32[64,4]{0,1:T(4,128)S(1)} %copy.27), kind=kOutput, calls=%fused_computation.28 | convolution fusion | flops 403046400 | bytes 3933188 | tf_op jit(solution)/shard_map/dot_general | solution.py:41
  78.3 1.1 %fusion.22 = bf16[1,64,4,512]{3,1,2,0:T(8,128)(2,1)S(1)} fusion(s32[]{:T(128)S(6)} %select_n.69, bf16[2048,576]{1,0:T(8,128)(2,1)S(1)} %copy-done.5, bf16[64,4,1536]{2,1,0:T(4,128)(2,1)S(1)} %dot_general.42, f32[64,4]{0,1:T(4,128)S(1)} %copy.23, f32[64,512]{1,0:T(8,128)S(1)} %copy-done.4, f32[64,4]{0,1:T(4,128)S(1)} %copy.22), kind=kOutput, calls=%fused_computation.29 | convolution fusion | flops 403177472 | bytes 3540996 | tf_op jit(solution)/shard_map/dot_general | solution.py:41
  79.3 0.1 maximum_bitcast_fusion
  79.4 1.2 %copy.28 = bf16[1,2,64,4,512]{4,3,2,1,0:T(4,128)(2,1)} copy(bf16[1,2,64,4,512]{4,2,3,1,0:T(8,128)(2,1)S(1)} %maximum_bitcast_fusion) | data formatting | bytes 1048576
  80.6 1.3 %fusion.71 = (f32[256]{0:T(256)S(1)}, f32[256,2048]{1,0:T(8,128)S(1)}) fusion(bf16[256,576]{1,0:T(8,128)(2,1)S(1)} %copy-done.3, bf16[2048,576]{1,0:T(8,128)(2,1)S(1)} %copy-done.5, s32[256]{0:T(256)S(1)} %le.16, s32[2048]{0:T(1024)S(1)} %fusion.52, s32[256]{0:T(256)S(1)} %eq.42), kind=kOutput, calls=%fused_computation.93 | convolution fusion | flops 607125248 | bytes 4762624 | tf_op jit(solution)/shard_map/dot_general | solution.py:85
  81.9 0.8 fusion.7
  82.7 0.9 fusion.28
  83.6 0.8 reshape.143
  (19 shorter events, 0.1 us)
Async XLA Ops:
  7.2 25.3 %copy-start = (bf16[1,2,64,4,576]{4,3,2,1,0:T(4,128)(2,1)S(1)}, bf16[1,2,64,4,576]{4,3,2,1,0:T(4,128)(2,1)}, u32[]{:S(2)}) copy-start(bf16[1,2,64,4,576]{4,3,2,1,0:T(4,128)(2,1)} %param.11) | copy-start | bytes 1769476
  7.2 25.1 %copy-start.1 = (bf16[1,2,64,576]{3,2,1,0:T(8,128)(2,1)S(1)}, bf16[1,2,64,576]{3,2,1,0:T(8,128)(2,1)}, u32[]{:S(2)}) copy-start(bf16[1,2,64,576]{3,2,1,0:T(8,128)(2,1)} %param.10) | copy-start | bytes 442372
  7.2 59.1 %all-gather.2.cloned.1.call-start = ((), (), s32[]{:S(2)}) async-start(), calls=%async_computation | async-start | bytes 3276800 | tf_op jit(solution)/shard_map/all_gather | solution.py:78
  32.0 1.7 %copy-start.2 = (bf16[64,4,576]{2,1,0:T(4,128)(2,1)S(1)}, bf16[64,4,576]{2,1,0:T(4,128)(2,1)}, u32[]{:S(2)}) copy-start(bf16[64,4,576]{2,1,0:T(4,128)(2,1)} %param.7) | copy-start | bytes 884740
  76.1 2.2 %copy-start.4 = (f32[64,512]{1,0:T(8,128)S(1)}, f32[64,512]{1,0:T(8,128)}, u32[]{:S(2)}) copy-start(f32[64,512]{1,0:T(8,128)} %fusion.47) | copy-start | bytes 393220
  76.1 2.2 %copy-start.5 = (bf16[2048,576]{1,0:T(8,128)(2,1)S(1)}, bf16[2048,576]{1,0:T(8,128)(2,1)}, u32[]{:S(2)}) copy-start(bf16[2048,576]{1,0:T(8,128)(2,1)} %all-gather.2.cloned.1.call-done) | copy-start | bytes 7077892
  79.3 1.3 %copy-start.3 = (bf16[256,576]{1,0:T(8,128)(2,1)S(1)}, bf16[256,576]{1,0:T(8,128)(2,1)}, u32[]{:S(2)}) copy-start(bf16[256,576]{1,0:T(8,128)(2,1)} %reshape.142) | copy-start | bytes 884740
Sparse Core Ops, SparseCore 0:
  25.6 40.6 all-gather.1
where the time goes:
time: 92 us; the launch traced here: 91.2 us
  waiting for transfers between devices  29.3 us (32%)
  blocking collectives  18.2 us (20%)
  between operations  16 us (17%)
  matrix products  12.7 us (14%)
  other arithmetic  8.67 us (9%)
  local copies, waits for them, and re-layouts  6.26 us (7%)
    all_gather x1, waiting for transfers between devices, body(): piece = lax.all_gather(block, 'ctx', axis=0, tiled=True)  29.2 us
    all_gather x1, blocking collectives, body(): block = lax.all_gather(latent_cache, 'ep', axis=0, tiled=True)  18.2 us
    dot_general x2, matrix products, decode_group(): lax.dot_general(flat, prefix, (((1,), (1,)), ((), ())), preferred_element...  5.99 us
    dot_general x2, matrix products, decode_group(): jnp.dot(prefix_weights.astype(jnp.bfloat16).reshape(count * heads, reach)...  3.19 us
    reduce_sum x2, other arithmetic, decode_group(): total = jnp.sum(prefix_weights, axis=2) + jnp.sum(own_weights, axis=2)  2.23 us
    reduce_sum x1, other arithmetic, body(): group_length = jnp.sum(jnp.where(owner, prompt_lengths, 0))  1.94 us
  transfers between devices with their start and end apart: 1, of which 1 were waited for; matrix products, arithmetic and copies ran while one was open for 11% of the time, Pallas kernels for 0%

commit v1 on v0

v1 whole, which is shorter than its diff:
```python
import functools
import math

import jax
import jax.numpy as jnp
from jax import lax
from jax.experimental import pallas as pl
from jax.experimental.pallas import tpu as pltpu
from jax.sharding import PartitionSpec as P

LAT = 512
SCALE = 192 ** (-0.5)
RATE = SCALE * math.log2(math.e)
FLOOR = -1e30
MESH = pl.DeviceIdType.MESH


def kernel(
    sizes,
    lengths_ref,
    group_ref,
    latent_ref,
    pq_ref,
    dq_ref,
    own_ref,
    pout_ref,
    dout_ref,
    cache,
    queries,
    acc,
    local_sem,
    send_sem,
    recv_sem,
):
    ctx_count, ep_count, heads, steps = sizes
    zs = ep_count // 2
    n2 = 2 if ctx_count % 2 == 0 else 1
    n1 = ctx_count // n2
    rows = latent_ref.shape[0]
    p_rows, d_rows = pq_ref.shape[0], dq_ref.shape[0]
    ctx = lax.axis_index("ctx")
    ep = lax.axis_index("ep")
    core = lax.rem(ep, 2)
    z = ep // 2
    i1, i2 = ctx // n2, lax.rem(ctx, n2)
    turn = core if n1 == n2 else 0
    na, nb = n2, n1
    fine = zs <= 4

    def column(a, b):
        o1 = b + turn * (a - b)
        o2 = a + turn * (b - a)
        return lax.rem(i1 + o1, n1) * n2 + lax.rem(i2 + o2, n2)

    def plane(dz):
        return lax.rem(z + dz, zs)

    sibling = (ctx, ep + 1 - 2 * core)
    z_peers = [(ctx, plane(dz) * 2 + core) for dz in range(1, zs)]
    a_peers = [(column(a, 0), ep) for a in range(1, na)]
    b_peers = [(column(0, b), ep) for b in range(1, nb)]

    barrier = pltpu.get_barrier_semaphore()
    partners = [sibling] + z_peers + a_peers + b_peers
    for peer in partners:
        pl.semaphore_signal(barrier, inc=1, device_id=peer, device_id_type=MESH)

    own_copy = pltpu.make_async_copy(latent_ref, cache.at[ctx, core, z], local_sem.at[0])
    own_copy.start()
    p_copy = pltpu.make_async_copy(pq_ref, queries.at[pl.ds(0, p_rows)], local_sem.at[1])
    p_copy.start()
    d_copy = pltpu.make_async_copy(dq_ref, queries.at[pl.ds(p_rows, d_rows)], local_sem.at[2])
    d_copy.start()
    pl.semaphore_wait(barrier, len(partners))

    sent = []

    def send(source, target, recv, peer):
        copy = pltpu.make_async_remote_copy(
            src_ref=source,
            dst_ref=target,
            send_sem=send_sem.at[len(sent)],
            recv_sem=recv,
            device_id=peer,
            device_id_type=MESH,
        )
        copy.start()
        sent.append(copy)

    def landed(target, recv):
        pltpu.make_async_remote_copy(
            src_ref=target,
            dst_ref=target,
            send_sem=send_sem.at[0],
            recv_sem=recv,
            device_id=sibling,
            device_id_type=MESH,
        ).wait_recv()

    def place(col, side, dz):
        if dz is None:
            return cache.at[col, side], recv_sem.at[col, side, 0]
        return cache.at[col, side, plane(dz)], recv_sem.at[col, side, plane(dz)]

    parts = list(range(zs)) if fine else [None]

    slot, recv = place(ctx, core, 0)
    for peer in z_peers:
        send(latent_ref, slot, recv, peer)

    def forward(source, col, dz, peers):
        target, recv = place(col, core, dz)
        for peer in peers:
            send(target if source is None else source, target, recv, peer)

    def own_column():
        if fine:
            forward(latent_ref, ctx, 0, b_peers + a_peers + [sibling])
            yield
            for dz in range(1, zs):
                landed(*place(ctx, core, dz))
                forward(None, ctx, dz, b_peers + a_peers + [sibling])
        else:
            yield
            for dz in range(1, zs):
                landed(*place(ctx, core, dz))
            forward(None, ctx, None, b_peers + a_peers + [sibling])

    def pass_on(col, peers):
        for dz in parts:
            landed(*place(col, core, dz))
            forward(None, col, dz, peers)

    def await_sibling(col):
        for dz in parts:
            landed(*place(col, 1 - core, dz))

    first = own_column()
    next(first)

    request_count = lengths_ref.shape[0]
    q_count = p_rows // heads
    span = q_count * ctx_count // request_count
    chosen = group_ref[ctx]
    row = lax.broadcasted_iota(jnp.int32, (p_rows, 1), 0)
    query_id = ctx * q_count + row // heads
    low = jnp.zeros((p_rows, 1), jnp.int32)
    high = jnp.zeros((p_rows, 1), jnp.int32)
    d_low = jnp.int32(0)
    d_high = jnp.int32(0)
    end = jnp.int32(0)
    for r in range(request_count):
        start = end
        end = start + lengths_ref[r]
        mine = (query_id >= r * span) & (query_id < (r + 1) * span)
        low = jnp.where(mine, start, low)
        high = jnp.where(mine, end - span + (query_id - r * span), high)
        d_low = jnp.where(chosen == r, start, d_low)
        d_high = jnp.where(chosen == r, end, d_high)

    block = p_rows
    blocks = (p_rows + d_rows) // block
    tops = [None] * blocks
    totals = [None] * blocks

    def lanes(x):
        out = x[:, :128]
        for i in range(1, x.shape[1] // 128):
            out = out + x[:, i * 128 : (i + 1) * 128]
        return out

    def attend(i, keys, allowed):
        span_i = pl.ds(i * block, block)
        scores = lax.dot_general(
            queries[span_i, :], keys, (((1,), (1,)), ((), ())), preferred_element_type=jnp.float32
        )
        scores = jnp.where(allowed, scores, FLOOR)
        top = jnp.max(scores, axis=1, keepdims=True)
        if tops[i] is not None:
            top = jnp.maximum(top, tops[i])
        weights = jnp.exp2((scores - top) * RATE)
        mixed = jnp.dot(
            weights.astype(jnp.bfloat16), keys[:, :LAT], preferred_element_type=jnp.float32
        )
        total = lanes(weights)
        if tops[i] is None:
            acc[span_i, :] = mixed
        else:
            keep = jnp.exp2((tops[i] - top) * RATE)
            acc[span_i, :] = acc[span_i, :] * keep + mixed
            total = total + totals[i] * keep
        tops[i], totals[i] = top, total

    def compute(col, side):
        keys = cache[col, side].reshape(zs * rows, cache.shape[-1])
        lane = lax.broadcasted_iota(jnp.int32, (1, zs * rows), 1)
        pos = col * (rows * ep_count) + (lane // rows * 2 + side) * rows + lane % rows
        attend(0, keys, (pos >= low) & (pos <= high))
        live = (pos >= d_low) & (pos < d_high)
        for i in range(1, blocks):
            attend(i, keys, live)

    p_copy.wait()
    d_copy.wait()
    count = own_ref.shape[0] // steps
    lane = lax.broadcasted_iota(jnp.int32, (1, own_ref.shape[0]), 1)
    for i in range(1, blocks):
        at = lax.broadcasted_iota(jnp.int32, (block, 1), 0) + (i - 1) * block
        token = at // heads
        same = (lane % count == token % count) & (lane // count <= token // count)
        attend(i, own_ref[...], same)

    own_copy.wait()
    for _ in first:
        pass
    compute(ctx, core)
    for a in range(1, na):
        pass_on(column(a, 0), b_peers + [sibling])
    await_sibling(ctx)
    compute(ctx, 1 - core)
    for a in range(1, na):
        compute(column(a, 0), core)
    if n1 == n2:
        theirs = [(b, a) for b in range(nb) for a in range(na) if (a, b) != (0, 0)]
        theirs = [(a, b) for b in range(nb) for a in range(na) if (a, b) != (0, 0)]
        theirs = [(b, a) for (a, b) in theirs]
    else:
        theirs = [(a, b) for b in range(nb) for a in range(na) if (a, b) != (0, 0)]
    mine = [(a, b) for b in range(1, nb) for a in range(na)]
    ahead = len(theirs) - len(mine)
    for a, b in theirs[:ahead]:
        await_sibling(column(a, b))
        compute(column(a, b), 1 - core)
    for (a, b), (c, d) in zip(mine, theirs[ahead:]):
        pass_on(column(a, b), [sibling])
        compute(column(a, b), core)
        await_sibling(column(c, d))
        compute(column(c, d), 1 - core)

    for i in range(blocks):
        total = jnp.sum(totals[i], axis=1, keepdims=True)
        out = (acc[pl.ds(i * block, block), :] / total).astype(jnp.bfloat16)
        if i == 0:
            pout_ref[...] = out
        else:
            dout_ref[pl.ds((i - 1) * block, block), :] = out
    for copy in sent:
        copy.wait_send()


def body(ctx_count, ep_count, latent, prefill_query, lengths, group_of, own, decode_query):
    rows, width = latent.shape
    q_count, heads, _ = prefill_query.shape
    _, steps, count, _, _ = decode_query.shape
    p_rows, d_rows = q_count * heads, steps * count * heads
    zs = ep_count // 2
    n2 = 2 if ctx_count % 2 == 0 else 1
    n1 = ctx_count // n2
    unit = zs if zs <= 4 else 1
    copies = (zs - 1) + unit * ((n2 - 1) + n2 * (n1 - 1) + ctx_count)
    smem = pl.BlockSpec(memory_space=pltpu.SMEM)
    anywhere = pl.BlockSpec(memory_space=pl.ANY)
    vmem = pl.BlockSpec(memory_space=pltpu.VMEM)
    pairs = (p_rows + d_rows) * (rows * ep_count * ctx_count + steps * count)
    prefill, decode = pl.pallas_call(
        functools.partial(kernel, (ctx_count, ep_count, heads, steps)),
        out_shape=(
            jax.ShapeDtypeStruct((p_rows, LAT), jnp.bfloat16),
            jax.ShapeDtypeStruct((d_rows, LAT), jnp.bfloat16),
        ),
        in_specs=[smem, smem, anywhere, anywhere, anywhere, vmem],
        out_specs=(vmem, vmem),
        scratch_shapes=[
            pltpu.VMEM((ctx_count, 2, zs, rows, width), jnp.bfloat16),
            pltpu.VMEM((p_rows + d_rows, width), jnp.bfloat16),
            pltpu.VMEM((p_rows + d_rows, LAT), jnp.float32),
            pltpu.SemaphoreType.DMA((3,)),
            pltpu.SemaphoreType.DMA((copies,)),
            pltpu.SemaphoreType.DMA((ctx_count, 2, zs)),
        ],
        compiler_params=pltpu.CompilerParams(
            collective_id=0, has_side_effects=True, vmem_limit_bytes=48 * 1024 * 1024
        ),
        cost_estimate=pl.CostEstimate(
            flops=2 * pairs * (width + LAT), bytes_accessed=4 << 20, transcendentals=pairs
        ),
    )(
        lengths,
        group_of,
        latent,
        prefill_query.reshape(p_rows, width),
        decode_query.reshape(d_rows, width),
        own.reshape(steps * count, width),
    )
    return (
        prefill.reshape(q_count, heads, LAT),
        decode.reshape(1, steps, count, heads, LAT),
    )


def solution(mesh):
    in_specs = (
        P(("ctx", "ep"), None),
        P("ctx", "ep", None),
        P(),
        P(),
        P("ctx", None, None, None),
        P("ctx", None, None, "ep", None),
    )
    out_specs = (P("ctx", "ep", None), P("ctx", None, None, "ep", None))
    whole = functools.partial(body, mesh.shape["ctx"], mesh.shape["ep"])
    return jax.shard_map(whole, mesh=mesh, in_specs=in_specs, out_specs=out_specs, check_vma=False)
```

time: 92 us -> 36.4 us (0.40)
  Pallas kernels: 0 us -> 31.6 us
  waiting for transfers between devices: 29.3 us -> 0 us
  blocking collectives: 18.2 us -> 0 us
  between operations: 16 us -> 0.7 us
  matrix products: 12.7 us -> 0 us
  other arithmetic: 8.67 us -> 0 us
  local copies, waits for them, and re-layouts: 6.26 us -> 3.82 us
    pallas_call x0 -> x1, Pallas kernels: none -> 31.6 us  [body(): pl.pallas_call(functools.partial(kernel, (ctx_count, ep_count, heads, ste...]
    all_gather x1 -> x0, waiting for transfers between devices: 29.2 us -> none  [body(): piece = lax.all_gather(block, 'ctx', axis=0, tiled=True)]
    all_gather x1 -> x0, blocking collectives: 18.2 us -> none  [body(): block = lax.all_gather(latent_cache, 'ep', axis=0, tiled=True)]
    dot_general x9 -> x0, matrix products: 12.7 us -> none  [the longest x2 5.99 us: decode_group(): lax.dot_general(flat, prefix, (((1,), (1,)), ((), ())), preferred_element...]
    reduce_sum x7 -> x0, other arithmetic: 6.4 us -> none  [the longest x2 2.23 us: decode_group(): total = jnp.sum(prefix_weights, axis=2) + jnp.sum(own_weights, axis=2)]
    reshape x2 -> x4, local copies, waits for them, and re-layouts: 1.64 us -> 3.2 us  [the longest x1 1.19 us: body(): prefill_query.reshape(p_rows, width)]
    another operation x4 -> x0, other arithmetic: 1.52 us -> none
    slice x2 -> x0, local copies, waits for them, and re-layouts: 1.32 us -> none  [the longest x1 1.3 us: decode_group(): query = queries[step]]
  transfers between devices with their start and end apart: 1 -> 0, of which waited for: 1 -> 0; matrix products, arithmetic and copies ran while one was open for 11% -> 0% of each run, Pallas kernels for 0% -> 0%
where the time goes in v1:
time: 36.4 us; the launch traced here: 36.1 us
  Pallas kernels  31.6 us (87%)
  local copies, waits for them, and re-layouts  3.82 us (10%)
  between operations  0.7 us (2%)
    pallas_call x1, Pallas kernels, body(): pl.pallas_call(functools.partial(kernel, (ctx_count, ep_count, heads, ste...  31.6 us
    reshape x1, local copies, waits for them, and re-layouts, body(): prefill_query.reshape(p_rows, width)  1.19 us
    reshape x1, local copies, waits for them, and re-layouts, body(): decode.reshape(1, steps, count, heads, LAT)  0.92 us
    reshape x1, local copies, waits for them, and re-layouts, body(): prefill.reshape(q_count, heads, LAT)  0.77 us

profile of v1, /device:TPU:0, one launch (start us, length us, event | category | flops | bytes accessed | tf_op | source)
XLA Modules:
  0.0 36.1 jit_solution(10786961454237230912)
XLA Ops:
  0.6 0.0 copy-start.4
  0.6 1.2 %reshape.19.pq_ref = bf16[256,576]{1,0:T(8,128)(2,1)S(1)} reshape(bf16[64,4,576]{2,1,0:T(4,128)(2,1)} %param.7) | data formatting | bytes 589824 | tf_op jit(solution)/shard_map/reshape | solution.py:291
  1.8 0.0 copy-done.4
  1.8 0.0 copy-start
  1.9 0.0 copy-start.1
  1.9 0.0 copy-start.2
  1.9 0.0 copy-start.3
  1.9 0.3 reshape.20.dq_ref
  2.2 0.5 %copy-done = bf16[1,2,64,576]{3,2,1,0:T(8,128)(2,1)S(1)} copy-done((bf16[1,2,64,576]{3,2,1,0:T(8,128)(2,1)S(1)}, bf16[1,2,64,576]{3,2,1,0:T(8,128)(2,1)}, u32[]{:S(2)}) %copy-start) | copy-done | bytes 147480
  2.8 0.1 copy-done.1
  2.8 0.0 copy-done.2
  2.8 0.0 copy-done.3
  2.8 31.6 %shard_map.77 = (bf16[256,512]{1,0:T(8,128)(2,1)S(1)}, bf16[512,512]{1,0:T(8,128)(2,1)S(1)}) custom-call(s32[2]{0:T(128)S(1)} %copy-done.2, s32[4]{0:T(128)S(1)} %copy-done.3, bf16[64,576]{1,0:T(8,128)(2,1)S(1)} %copy-done.1, bf16[256,576]{1,0:T(8,128)(2,1)S(1)} %reshape.19.pq_ref, bf16[512,576]{1,0:T(8,128)(2,1)S(1)} %reshape.20.dq_ref, ...), custom_call_target="tpu_custom_call" | custom-call | flops 3636461568 | bytes 4194304 | tf_op jit(solution)/shard_map/pallas_call | solution.py:265
  34.4 0.8 %reshape.22 = bf16[64,4,512]{2,1,0:T(4,128)(2,1)} reshape(bf16[256,512]{1,0:T(8,128)(2,1)S(1)} %get-tuple-element.4) | data formatting | bytes 524288 | tf_op jit(solution)/shard_map/reshape | solution.py:296
  35.2 0.9 %reshape.23 = bf16[1,2,64,4,512]{4,3,2,1,0:T(4,128)(2,1)} reshape(bf16[512,512]{1,0:T(8,128)(2,1)S(1)} %get-tuple-element.5) | data formatting | bytes 1048576 | tf_op jit(solution)/shard_map/reshape | solution.py:297
Async XLA Ops:
  0.6 1.2 %copy-start.4 = (bf16[1,2,64,4,576]{4,3,2,1,0:T(4,128)(2,1)S(1)}, bf16[1,2,64,4,576]{4,3,2,1,0:T(4,128)(2,1)}, u32[]{:S(2)}) copy-start(bf16[1,2,64,4,576]{4,3,2,1,0:T(4,128)(2,1)} %param.11) | copy-start | bytes 1769476
  1.8 0.9 %copy-start = (bf16[1,2,64,576]{3,2,1,0:T(8,128)(2,1)S(1)}, bf16[1,2,64,576]{3,2,1,0:T(8,128)(2,1)}, u32[]{:S(2)}) copy-start(bf16[1,2,64,576]{3,2,1,0:T(8,128)(2,1)} %param.10) | copy-start | bytes 442372
  1.9 1.0 %copy-start.1 = (bf16[64,576]{1,0:T(8,128)(2,1)S(1)}, bf16[64,576]{1,0:T(8,128)(2,1)}, u32[]{:S(2)}) copy-start(bf16[64,576]{1,0:T(8,128)(2,1)} %latent_ref.1) | copy-start | bytes 221188
  1.9 1.0 %copy-start.2 = (s32[2]{0:T(128)S(1)}, s32[2]{0:T(128)}, u32[]{:S(2)}) copy-start(s32[2]{0:T(128)} %lengths_ref.1) | copy-start | bytes 28
  1.9 0.9 %copy-start.3 = (s32[4]{0:T(128)S(1)}, s32[4]{0:T(128)}, u32[]{:S(2)}) copy-start(s32[4]{0:T(128)} %group_ref.1) | copy-start | bytes 52

commit v2 on v1

v2 whole, which is shorter than its diff:
```python
import functools
import math

import jax
import jax.numpy as jnp
from jax import lax
from jax.experimental import pallas as pl
from jax.experimental.pallas import tpu as pltpu
from jax.sharding import PartitionSpec as P

LAT = 512
SCALE = 192 ** (-0.5)
RATE = SCALE * math.log2(math.e)
FLOOR = -1e30
MESH = pl.DeviceIdType.MESH


def layout(rows):
    halves = 2 if rows % 32 == 0 else 1
    return halves, 4 * rows + rows // halves


def kernel(
    sizes,
    lengths_ref,
    group_ref,
    latent_ref,
    pq_ref,
    dq_ref,
    own_ref,
    pout_ref,
    dout_ref,
    cache,
    pq_raw,
    dq_raw,
    queries,
    tails,
    acc,
    local_sem,
    send_sem,
    recv_sem,
):
    ctx_count, ep_count, heads, steps = sizes
    zs = ep_count // 2
    n2 = 2 if ctx_count % 2 == 0 else 1
    n1 = ctx_count // n2
    rows, width = latent_ref.shape
    halves, packed = layout(rows)
    half = rows // halves
    rope = width - LAT
    p_rows, d_rows = pout_ref.shape[0], dout_ref.shape[0]
    ctx = lax.axis_index("ctx")
    ep = lax.axis_index("ep")
    core = lax.rem(ep, 2)
    z = ep // 2
    i1, i2 = ctx // n2, lax.rem(ctx, n2)
    turn = core if n1 == n2 else 0
    na, nb = n2, n1
    line = zs == 4

    def column(a, b):
        o1 = b + turn * (a - b)
        o2 = a + turn * (b - a)
        return lax.rem(i1 + o1, n1) * n2 + lax.rem(i2 + o2, n2)

    flip = z // 2 if line else 0
    near = z + flip * (3 - 2 * z)

    def mirror(p):
        return p + flip * (3 - 2 * p)

    if line:
        planes = [z, mirror(1 - near), mirror(2), mirror(3)]
    else:
        planes = [lax.rem(z + dz, zs) for dz in range(zs)]

    def there(p):
        return (ctx, p * 2 + core)

    sibling = (ctx, ep + 1 - 2 * core)
    z_peers = [there(p) for p in planes[1:]]
    a_peers = [(column(a, 0), ep) for a in range(1, na)]
    b_peers = [(column(0, b), ep) for b in range(1, nb)]

    barrier = pltpu.get_barrier_semaphore()
    partners = [sibling] + z_peers + a_peers + b_peers
    for peer in partners:
        pl.semaphore_signal(barrier, inc=1, device_id=peer, device_id_type=MESH)

    p_copy = pltpu.make_async_copy(pq_ref, pq_raw, local_sem.at[0])
    p_copy.start()
    d_copy = pltpu.make_async_copy(dq_ref, dq_raw, local_sem.at[1])
    d_copy.start()
    for j in range(LAT // 128):
        cache[ctx, ep, pl.ds(j * rows, rows), :] = latent_ref[:, j * 128 : (j + 1) * 128]
    last = latent_ref[:, LAT:]
    if halves == 2:
        last = jnp.concatenate([last[:half], last[half:]], axis=1)
    else:
        last = jnp.concatenate([last, jnp.zeros_like(last)], axis=1)
    cache[ctx, ep, pl.ds(4 * rows, half), :] = last
    pl.semaphore_wait(barrier, len(partners))

    sent, sent_inner, used = [], [], [0]

    def link(col, index, peer):
        slot = cache.at[col, index]
        copy = pltpu.make_async_remote_copy(
            src_ref=slot,
            dst_ref=slot,
            send_sem=send_sem.at[used[0]],
            recv_sem=recv_sem.at[col, index],
            device_id=peer,
            device_id_type=MESH,
        )
        used[0] += 1
        return copy

    def landed(col, index):
        slot = cache.at[col, index]
        pltpu.make_async_remote_copy(
            src_ref=slot,
            dst_ref=slot,
            send_sem=send_sem.at[0],
            recv_sem=recv_sem.at[col, index],
            device_id=sibling,
            device_id_type=MESH,
        ).wait_recv()

    def forward(col, index, peers):
        for peer in peers:
            sent.append(link(col, index, peer))
            sent[-1].start()

    inner = near == 1
    if line:
        forward(ctx, ep, [there(mirror(near + 1))])
        sent_inner.append(link(ctx, ep, there(mirror(0))))
        pl.when(inner)(sent_inner[-1].start)
    else:
        forward(ctx, ep, z_peers)
    forward(ctx, ep, a_peers + b_peers + [sibling])

    def pass_on(col, i, peers):
        index = planes[i] * 2 + core
        landed(col, index)
        if line and col is ctx:
            goal = 2 if i == 1 else 0
            sent_inner.append(link(ctx, index, there(mirror(goal))))
            pl.when(inner)(sent_inner[-1].start)
        forward(col, index, peers)

    def await_sibling(col):
        for p in planes:
            landed(col, p * 2 + 1 - core)

    p_copy.wait()
    d_copy.wait()
    blank = jnp.zeros((p_rows, rope), jnp.bfloat16)
    block = p_rows
    blocks = (p_rows + d_rows) // block
    for i in range(blocks):
        if i == 0:
            raw = pq_raw[...]
        else:
            tokens = block // heads
            raw = dq_raw[pl.ds((i - 1) * tokens, tokens), :, :]
        raw = raw.reshape(block, width)
        at = pl.ds(i * block, block)
        queries[at, :] = raw[:, :LAT]
        tails[0, at, :] = jnp.concatenate([raw[:, LAT:], blank], axis=1)
        if halves == 2:
            tails[1, at, :] = jnp.concatenate([blank, raw[:, LAT:]], axis=1)

    request_count = lengths_ref.shape[0]
    q_count = p_rows // heads
    span = q_count * ctx_count // request_count
    chosen = group_ref[ctx]
    row = lax.broadcasted_iota(jnp.int32, (p_rows, 1), 0)
    query_id = ctx * q_count + row // heads
    low = jnp.zeros((p_rows, 1), jnp.int32)
    high = jnp.zeros((p_rows, 1), jnp.int32)
    d_low = jnp.int32(0)
    d_high = jnp.int32(0)
    end = jnp.int32(0)
    for r in range(request_count):
        start = end
        end = start + lengths_ref[r]
        mine = (query_id >= r * span) & (query_id < (r + 1) * span)
        low = jnp.where(mine, start, low)
        high = jnp.where(mine, end - span + (query_id - r * span), high)
        d_low = jnp.where(chosen == r, start, d_low)
        d_high = jnp.where(chosen == r, end, d_high)

    tops = [None] * blocks
    totals = [None] * blocks

    def lanes(x):
        out = x[:, :128]
        for i in range(1, x.shape[1] // 128):
            out = out + x[:, i * 128 : (i + 1) * 128]
        return out

    def attend(i, keys, values, allowed):
        at = pl.ds(i * block, block)
        scores = []
        for h, part in enumerate(keys):
            query = jnp.concatenate([queries[at, :], tails[h, at, :]], axis=1)
            scores.append(
                lax.dot_general(
                    query, part, (((1,), (1,)), ((), ())), preferred_element_type=jnp.float32
                )
            )
        scores = scores[0] if len(scores) == 1 else jnp.concatenate(scores, axis=1)
        scores = jnp.where(allowed, scores, FLOOR)
        top = jnp.max(scores, axis=1, keepdims=True)
        if tops[i] is not None:
            top = jnp.maximum(top, tops[i])
        weights = jnp.exp2((scores - top) * RATE)
        mixed = jnp.dot(
            weights.astype(jnp.bfloat16), values, preferred_element_type=jnp.float32
        )
        total = lanes(weights)
        if tops[i] is None:
            acc[at, :] = mixed
        else:
            keep = jnp.exp2((tops[i] - top) * RATE)
            acc[at, :] = acc[at, :] * keep + mixed
            total = total + totals[i] * keep
        tops[i], totals[i] = top, total

    def compute(col):
        keys, values = [], []
        count = ep_count * half
        for h in range(halves):
            tiles = [
                cache[col, :, pl.ds(j * rows + h * half, half), :].reshape(count, 128)
                for j in range(LAT // 128)
            ]
            tiles.append(cache[col, :, pl.ds(4 * rows, half), :].reshape(count, 128))
            keys.append(jnp.concatenate(tiles, axis=1))
            values.append(keys[-1][:, :LAT])
        values = values[0] if halves == 1 else jnp.concatenate(values, axis=0)
        lane = lax.broadcasted_iota(jnp.int32, (1, halves * count), 1)
        within = lane % count
        pos = (within // half) * rows + (lane // count) * half + within % half
        pos = pos + col * (rows * ep_count)
        attend(0, keys, values, (pos >= low) & (pos <= high))
        live = (pos >= d_low) & (pos < d_high)
        for i in range(1, blocks):
            attend(i, keys, values, live)

    def own_rows():
        count = own_ref.shape[0] // steps
        lane = lax.broadcasted_iota(jnp.int32, (1, own_ref.shape[0]), 1)
        own = own_ref[...]
        own_keys = jnp.concatenate([own, jnp.zeros((own.shape[0], rope), jnp.bfloat16)], axis=1)
        for i in range(1, blocks):
            at = lax.broadcasted_iota(jnp.int32, (block, 1), 0) + (i - 1) * block
            token = at // heads
            same = (lane % count == token % count) & (lane // count <= token // count)
            attend(i, [own_keys], own[:, :LAT], same)

    first = [(a, 0) for a in range(1, na)]
    second = [(0, b) for b in range(1, nb)]
    third = [(a, b) for b in range(1, nb) for a in range(1, na)]
    for i in range(zs + 1):
        if 1 <= i < zs:
            pass_on(ctx, i, a_peers + b_peers + [sibling])
        if i >= 1:
            for a, b in first:
                pass_on(column(a, b), i - 1, b_peers + [sibling])
        if i == 1:
            own_rows()
    await_sibling(ctx)
    compute(ctx)
    for a, b in second:
        for i in range(zs):
            pass_on(column(a, b), i, [sibling])
    for a, b in second + first:
        await_sibling(column(a, b))
        compute(column(a, b))
    for a, b in third:
        for i in range(zs):
            pass_on(column(a, b), i, [sibling])
        await_sibling(column(a, b))
        compute(column(a, b))

    for i in range(blocks):
        total = jnp.sum(totals[i], axis=1, keepdims=True)
        out = (acc[pl.ds(i * block, block), :] / total).astype(jnp.bfloat16)
        if i == 0:
            pout_ref[...] = out
        else:
            dout_ref[pl.ds((i - 1) * block, block), :] = out
    for copy in sent:
        copy.wait_send()
    for copy in sent_inner:
        pl.when(inner)(copy.wait_send)


def body(ctx_count, ep_count, latent, prefill_query, lengths, group_of, own, decode_query):
    rows, width = latent.shape
    q_count, heads, _ = prefill_query.shape
    _, steps, count, _, _ = decode_query.shape
    p_rows, d_rows = q_count * heads, steps * count * heads
    all_rows = p_rows + d_rows
    zs = ep_count // 2
    n2 = 2 if ctx_count % 2 == 0 else 1
    n1 = ctx_count // n2
    halves, packed = layout(rows)
    copies = 2 * zs + zs * ((n2 - 1) + n2 * (n1 - 1) + ctx_count)
    smem = pl.BlockSpec(memory_space=pltpu.SMEM)
    anywhere = pl.BlockSpec(memory_space=pl.ANY)
    vmem = pl.BlockSpec(memory_space=pltpu.VMEM)
    pairs = all_rows * (rows * ep_count * ctx_count + steps * count)
    prefill, decode = pl.pallas_call(
        functools.partial(kernel, (ctx_count, ep_count, heads, steps)),
        out_shape=(
            jax.ShapeDtypeStruct((p_rows, LAT), jnp.bfloat16),
            jax.ShapeDtypeStruct((d_rows, LAT), jnp.bfloat16),
        ),
        in_specs=[smem, smem, vmem, anywhere, anywhere, vmem],
        out_specs=(vmem, vmem),
        scratch_shapes=[
            pltpu.VMEM((ctx_count, ep_count, packed, 128), jnp.bfloat16),
            pltpu.VMEM((q_count, heads, width), jnp.bfloat16),
            pltpu.VMEM((steps * count, heads, width), jnp.bfloat16),
            pltpu.VMEM((all_rows, LAT), jnp.bfloat16),
            pltpu.VMEM((halves, all_rows, 128), jnp.bfloat16),
            pltpu.VMEM((all_rows, LAT), jnp.float32),
            pltpu.SemaphoreType.DMA((2,)),
            pltpu.SemaphoreType.DMA((copies,)),
            pltpu.SemaphoreType.DMA((ctx_count, ep_count)),
        ],
        compiler_params=pltpu.CompilerParams(
            collective_id=0, has_side_effects=True, vmem_limit_bytes=48 * 1024 * 1024
        ),
        cost_estimate=pl.CostEstimate(
            flops=2 * pairs * (width + LAT), bytes_accessed=4 << 20, transcendentals=pairs
        ),
    )(
        lengths,
        group_of,
        latent,
        prefill_query,
        decode_query.reshape(steps * count, heads, width),
        own.reshape(steps * count, width),
    )
    return (
        prefill.reshape(q_count, heads, LAT),
        decode.reshape(1, steps, count, heads, LAT),
    )


def solution(mesh):
    in_specs = (
        P(("ctx", "ep"), None),
        P("ctx", "ep", None),
        P(),
        P(),
        P("ctx", None, None, None),
        P("ctx", None, None, "ep", None),
    )
    out_specs = (P("ctx", "ep", None), P("ctx", None, None, "ep", None))
    whole = functools.partial(body, mesh.shape["ctx"], mesh.shape["ep"])
    return jax.shard_map(whole, mesh=mesh, in_specs=in_specs, out_specs=out_specs, check_vma=False)
```

time: 36.4 us -> 36.2 us (level)
  Pallas kernels: 31.6 us -> 28.8 us
  local copies, waits for them, and re-layouts: 3.82 us -> 6.2 us
    unnamed x10 -> x12, local copies, waits for them, and re-layouts: 0.62 us -> 4.52 us
    pallas_call x1, Pallas kernels: 31.6 us -> 28.8 us  [body(): pl.pallas_call(functools.partial(kernel, (ctx_count, ep_count, heads, ste...]
    reshape x2 -> x0, local copies, waits for them, and re-layouts: 1.52 us -> none  [the longest x1 1.19 us: body(): prefill_query.reshape(p_rows, width)]
where the time goes in v2:
time: 36.2 us; the launch traced here: 35.7 us
  Pallas kernels  28.8 us (80%)
  local copies, waits for them, and re-layouts  6.2 us (17%)
  between operations  0.66 us (2%)
    pallas_call x1, Pallas kernels, body(): pl.pallas_call(functools.partial(kernel, (ctx_count, ep_count, heads, ste...  28.8 us
    unnamed x12, local copies, waits for them, and re-layouts  4.52 us
    reshape x1, local copies, waits for them, and re-layouts, body(): decode.reshape(1, steps, count, heads, LAT)  0.92 us
    reshape x1, local copies, waits for them, and re-layouts, body(): prefill.reshape(q_count, heads, LAT)  0.77 us

profile of v2, /device:TPU:0, one launch (start us, length us, event | category | flops | bytes accessed | tf_op | source)
XLA Modules:
  0.0 35.7 jit_solution(11477789155317456521)
XLA Ops:
  0.6 0.0 copy-start.4
  0.6 0.0 copy-start.5
  0.7 0.6 %copy-done.4 = s32[2]{0:T(128)S(1)} copy-done((s32[2]{0:T(128)S(1)}, s32[2]{0:T(128)}, u32[]{:S(2)}) %copy-start.4) | copy-done | bytes 32
  1.3 0.0 copy-done.5
  1.3 0.0 copy-start
  1.3 1.1 %copy-done = bf16[1,2,64,4,576]{4,3,2,1,0:T(4,128)(2,1)S(1)} copy-done((bf16[1,2,64,4,576]{4,3,2,1,0:T(4,128)(2,1)S(1)}, bf16[1,2,64,4,576]{4,3,2,1,0:T(4,128)(2,1)}, u32[]{:S(2)}) %copy-start) | copy-done | bytes 589848
  2.4 0.0 copy-start.1
  2.4 1.0 %copy-done.1 = bf16[64,4,576]{2,1,0:T(4,128)(2,1)S(1)} copy-done((bf16[64,4,576]{2,1,0:T(4,128)(2,1)S(1)}, bf16[64,4,576]{2,1,0:T(4,128)(2,1)}, u32[]{:S(2)}) %copy-start.1) | copy-done | bytes 294936
  3.4 0.0 copy-start.2
  3.4 0.9 %copy-done.2 = bf16[1,2,64,576]{3,2,1,0:T(8,128)(2,1)S(1)} copy-done((bf16[1,2,64,576]{3,2,1,0:T(8,128)(2,1)S(1)}, bf16[1,2,64,576]{3,2,1,0:T(8,128)(2,1)}, u32[]{:S(2)}) %copy-start.2) | copy-done | bytes 147480
  4.3 0.0 copy-start.3
  4.3 0.9 %copy-done.3 = bf16[64,576]{1,0:T(8,128)(2,1)S(1)} copy-done((bf16[64,576]{1,0:T(8,128)(2,1)S(1)}, bf16[64,576]{1,0:T(8,128)(2,1)}, u32[]{:S(2)}) %copy-start.3) | copy-done | bytes 73752
  5.2 28.8 %shard_map.77 = (bf16[256,512]{1,0:T(8,128)(2,1)S(1)}, bf16[512,512]{1,0:T(8,128)(2,1)S(1)}) custom-call(s32[2]{0:T(128)S(1)} %copy-done.4, s32[4]{0:T(128)S(1)} %copy-done.5, bf16[64,576]{1,0:T(8,128)(2,1)S(1)} %copy-done.3, bf16[64,4,576]{2,1,0:T(4,128)(2,1)S(1)} %copy-done.1, bf16[128,4,576]{2,1,0:T(4,128)(2,1)S(1)} %bitcast.2, bf16[128,576]{1,0:T(8,128)(2,1)S(1)} %bitcast.3), custom_call_target="tpu_custom_call" | custom-call | flops 3636461568 | bytes 4194304 | tf_op jit(solution)/shard_map/pallas_call | solution.py:317
  34.0 0.8 %reshape.18 = bf16[64,4,512]{2,1,0:T(4,128)(2,1)} reshape(bf16[256,512]{1,0:T(8,128)(2,1)S(1)} %get-tuple-element.4) | data formatting | bytes 524288 | tf_op jit(solution)/shard_map/reshape | solution.py:351
  34.8 0.9 %reshape.19 = bf16[1,2,64,4,512]{4,3,2,1,0:T(4,128)(2,1)} reshape(bf16[512,512]{1,0:T(8,128)(2,1)S(1)} %get-tuple-element.5) | data formatting | bytes 1048576 | tf_op jit(solution)/shard_map/reshape | solution.py:352
Async XLA Ops:
  0.6 0.7 %copy-start.4 = (s32[2]{0:T(128)S(1)}, s32[2]{0:T(128)}, u32[]{:S(2)}) copy-start(s32[2]{0:T(128)} %lengths_ref.1) | copy-start | bytes 28
  0.6 0.7 %copy-start.5 = (s32[4]{0:T(128)S(1)}, s32[4]{0:T(128)}, u32[]{:S(2)}) copy-start(s32[4]{0:T(128)} %group_ref.1) | copy-start | bytes 52
  1.3 1.1 %copy-start = (bf16[1,2,64,4,576]{4,3,2,1,0:T(4,128)(2,1)S(1)}, bf16[1,2,64,4,576]{4,3,2,1,0:T(4,128)(2,1)}, u32[]{:S(2)}) copy-start(bf16[1,2,64,4,576]{4,3,2,1,0:T(4,128)(2,1)} %param.11) | copy-start | bytes 1769476
  2.4 1.0 %copy-start.1 = (bf16[64,4,576]{2,1,0:T(4,128)(2,1)S(1)}, bf16[64,4,576]{2,1,0:T(4,128)(2,1)}, u32[]{:S(2)}) copy-start(bf16[64,4,576]{2,1,0:T(4,128)(2,1)} %pq_ref.1) | copy-start | bytes 884740
  3.4 0.9 %copy-start.2 = (bf16[1,2,64,576]{3,2,1,0:T(8,128)(2,1)S(1)}, bf16[1,2,64,576]{3,2,1,0:T(8,128)(2,1)}, u32[]{:S(2)}) copy-start(bf16[1,2,64,576]{3,2,1,0:T(8,128)(2,1)} %param.10) | copy-start | bytes 442372
  4.3 0.9 %copy-start.3 = (bf16[64,576]{1,0:T(8,128)(2,1)S(1)}, bf16[64,576]{1,0:T(8,128)(2,1)}, u32[]{:S(2)}) copy-start(bf16[64,576]{1,0:T(8,128)(2,1)} %latent_ref.1) | copy-start | bytes 221188

commit v3 on v2

--- a/solution.py
+++ b/solution.py
@@ -16,8 +16,10 @@
 
 
 def layout(rows):
+    subs = 2 if rows % 64 == 0 else 1
+    rows = rows // subs
     halves = 2 if rows % 32 == 0 else 1
-    return halves, 4 * rows + rows // halves
+    return subs, halves, 4 * rows + rows // halves
 
 
 def kernel(
@@ -31,6 +33,8 @@
     pout_ref,
     dout_ref,
     cache,
+    latent_raw,
+    own_raw,
     pq_raw,
     dq_raw,
     queries,
@@ -44,8 +48,9 @@
     zs = ep_count // 2
     n2 = 2 if ctx_count % 2 == 0 else 1
     n1 = ctx_count // n2
-    rows, width = latent_ref.shape
-    halves, packed = layout(rows)
+    shard, width = latent_ref.shape
+    subs, halves, packed = layout(shard)
+    rows = shard // subs
     half = rows // halves
     rope = width - LAT
     p_rows, d_rows = pout_ref.shape[0], dout_ref.shape[0]
@@ -87,75 +92,73 @@
     for peer in partners:
         pl.semaphore_signal(barrier, inc=1, device_id=peer, device_id_type=MESH)
 
-    p_copy = pltpu.make_async_copy(pq_ref, pq_raw, local_sem.at[0])
-    p_copy.start()
-    d_copy = pltpu.make_async_copy(dq_ref, dq_raw, local_sem.at[1])
-    d_copy.start()
-    for j in range(LAT // 128):
-        cache[ctx, ep, pl.ds(j * rows, rows), :] = latent_ref[:, j * 128 : (j + 1) * 128]
-    last = latent_ref[:, LAT:]
-    if halves == 2:
-        last = jnp.concatenate([last[:half], last[half:]], axis=1)
-    else:
-        last = jnp.concatenate([last, jnp.zeros_like(last)], axis=1)
-    cache[ctx, ep, pl.ds(4 * rows, half), :] = last
+    copies = [
+        pltpu.make_async_copy(source, target, local_sem.at[i])
+        for i, (source, target) in enumerate(
+            [(latent_ref, latent_raw), (pq_ref, pq_raw), (dq_ref, dq_raw), (own_ref, own_raw)]
+        )
+    ]
+    for copy in copies:
+        copy.start()
+    copies[0].wait()
+    for sub in range(subs):
+        base = sub * rows
+        for j in range(LAT // 128):
+            tile = latent_raw[base : base + rows, j * 128 : (j + 1) * 128]
+            cache[sub, ctx, ep, pl.ds(j * rows, rows), :] = tile
+        last = latent_raw[base : base + rows, LAT:]
+        if halves == 2:
+            last = jnp.concatenate([last[:half], last[half:]], axis=1)
+        else:
+            last = jnp.concatenate([last, jnp.zeros_like(last)], axis=1)
+        cache[sub, ctx, ep, pl.ds(4 * rows, half), :] = last
     pl.semaphore_wait(barrier, len(partners))
 
-    sent, sent_inner, used = [], [], [0]
-
-    def link(col, index, peer):
-        slot = cache.at[col, index]
-        copy = pltpu.make_async_remote_copy(
+    sent = []
+
+    def link(sub, col, index, peer):
+        slot = cache.at[sub, col, index]
+        return pltpu.make_async_remote_copy(
             src_ref=slot,
             dst_ref=slot,
-            send_sem=send_sem.at[used[0]],
-            recv_sem=recv_sem.at[col, index],
+            send_sem=send_sem.at[len(sent)],
+            recv_sem=recv_sem.at[sub, col, index],
             device_id=peer,
             device_id_type=MESH,
         )
-        used[0] += 1
-        return copy
-
-    def landed(col, index):
-        slot = cache.at[col, index]
+
+    def landed(sub, col, index):
+        slot = cache.at[sub, col, index]
         pltpu.make_async_remote_copy(
             src_ref=slot,
             dst_ref=slot,
             send_sem=send_sem.at[0],
-            recv_sem=recv_sem.at[col, index],
+            recv_sem=recv_sem.at[sub, col, index],
             device_id=sibling,
             device_id_type=MESH,
         ).wait_recv()
 
-    def forward(col, index, peers):
+    def forward(sub, col, index, peers):
         for peer in peers:
-            sent.append(link(col, index, peer))
+            sent.append(link(sub, col, index, peer))
             sent[-1].start()
 
-    inner = near == 1
-    if line:
-        forward(ctx, ep, [there(mirror(near + 1))])
-        sent_inner.append(link(ctx, ep, there(mirror(0))))
-        pl.when(inner)(sent_inner[-1].start)
-    else:
-        forward(ctx, ep, z_peers)
-    forward(ctx, ep, a_peers + b_peers + [sibling])
-
-    def pass_on(col, i, peers):
+    forward(0, ctx, ep, z_peers)
+    early = list(sent)
+    for sub in range(subs):
+        forward(sub, ctx, ep, a_peers + b_peers + [sibling])
+
+    def pass_on(sub, col, i, peers):
         index = planes[i] * 2 + core
-        landed(col, index)
-        if line and col is ctx:
-            goal = 2 if i == 1 else 0
-            sent_inner.append(link(ctx, index, there(mirror(goal))))
-            pl.when(inner)(sent_inner[-1].start)
-        forward(col, index, peers)
-
-    def await_sibling(col):
+        landed(sub, col, index)
+        forward(sub, col, index, peers)
+
+    def await_sibling(sub, col):
         for p in planes:
-            landed(col, p * 2 + 1 - core)
-
-    p_copy.wait()
-    d_copy.wait()
+            landed(sub, col, p * 2 + 1 - core)
+
+    for copy in copies[1:]:
+        copy.wait()
     blank = jnp.zeros((p_rows, rope), jnp.bfloat16)
     block = p_rows
     blocks = (p_rows + d_rows) // block
@@ -229,31 +232,36 @@
             total = total + totals[i] * keep
         tops[i], totals[i] = top, total
 
-    def compute(col):
-        keys, values = [], []
+    def compute(items):
+        keys, values, pos = [], [], []
         count = ep_count * half
+        lane = lax.broadcasted_iota(jnp.int32, (1, count), 1)
+        within = (lane // half) * shard + lane % half
+
+        def tile(sub, col, first):
+            return cache[sub, col, :, pl.ds(first, half), :].reshape(count, 128)
+
         for h in range(halves):
-            tiles = [
-                cache[col, :, pl.ds(j * rows + h * half, half), :].reshape(count, 128)
-                for j in range(LAT // 128)
-            ]
-            tiles.append(cache[col, :, pl.ds(4 * rows, half), :].reshape(count, 128))
-            keys.append(jnp.concatenate(tiles, axis=1))
-            values.append(keys[-1][:, :LAT])
+            blocks_of = []
+            for sub, col in items:
+                tiles = [tile(sub, col, j * rows + h * half) for j in range(LAT // 128)]
+                tiles.append(tile(sub, col, 4 * rows))
+                blocks_of.append(jnp.concatenate(tiles, axis=1))
+                pos.append(within + (col * (shard * ep_count) + sub * rows + h * half))
+            both = blocks_of[0] if len(blocks_of) == 1 else jnp.concatenate(blocks_of, axis=0)
+            keys.append(both)
+            values.append(both[:, :LAT])
         values = values[0] if halves == 1 else jnp.concatenate(values, axis=0)
-        lane = lax.broadcasted_iota(jnp.int32, (1, halves * count), 1)
-        within = lane % count
-        pos = (within // half) * rows + (lane // count) * half + within % half
-        pos = pos + col * (rows * ep_count)
+        pos = pos[0] if len(pos) == 1 else jnp.concatenate(pos, axis=1)
         attend(0, keys, values, (pos >= low) & (pos <= high))
         live = (pos >= d_low) & (pos < d_high)
         for i in range(1, blocks):
             attend(i, keys, values, live)
 
     def own_rows():
-        count = own_ref.shape[0] // steps
-        lane = lax.broadcasted_iota(jnp.int32, (1, own_ref.shape[0]), 1)
-        own = own_ref[...]
+        count = own_raw.shape[0] // steps
+        lane = lax.broadcasted_iota(jnp.int32, (1, own_raw.shape[0]), 1)
+        own = own_raw[...]
         own_keys = jnp.concatenate([own, jnp.zeros((own.shape[0], rope), jnp.bfloat16)], axis=1)
         for i in range(1, blocks):
             at = lax.broadcasted_iota(jnp.int32, (block, 1), 0) + (i - 1) * block
@@ -264,27 +272,50 @@
     first = [(a, 0) for a in range(1, na)]
     second = [(0, b) for b in range(1, nb)]
     third = [(a, b) for b in range(1, nb) for a in range(1, na)]
-    for i in range(zs + 1):
-        if 1 <= i < zs:
-            pass_on(ctx, i, a_peers + b_peers + [sibling])
-        if i >= 1:
-            for a, b in first:
-                pass_on(column(a, b), i - 1, b_peers + [sibling])
-        if i == 1:
-            own_rows()
-    await_sibling(ctx)
-    compute(ctx)
-    for a, b in second:
-        for i in range(zs):
-            pass_on(column(a, b), i, [sibling])
-    for a, b in second + first:
-        await_sibling(column(a, b))
-        compute(column(a, b))
-    for a, b in third:
-        for i in range(zs):
-            pass_on(column(a, b), i, [sibling])
-        await_sibling(column(a, b))
-        compute(column(a, b))
+    def planes_in(sub):
+        for i in range(1, zs):
+            pass_on(sub, ctx, i, a_peers + b_peers + [sibling])
+
+    def columns_in(sub, where, peers):
+        for a, b in where:
+            for i in range(zs):
+                pass_on(sub, column(a, b), i, peers)
+
+    def ready(items):
+        for sub, col in items:
+            await_sibling(sub, col)
+        compute(items)
+
+    own_rows()
+    for copy in early:
+        copy.wait_send()
+    for sub in range(1, subs):
+        forward(sub, ctx, ep, z_peers)
+    planes_in(0)
+    if subs == 2 and len(first) == len(second) == len(third) == 1:
+        fa, fb, fc = column(*first[0]), column(*second[0]), column(*third[0])
+        ready([(0, ctx)])
+        planes_in(1)
+        columns_in(0, first, b_peers + [sibling])
+        ready([(1, ctx)])
+        columns_in(0, second, [sibling])
+        ready([(0, fa), (0, fb)])
+        columns_in(1, first, b_peers + [sibling])
+        columns_in(0, third, [sibling])
+        columns_in(1, second, [sibling])
+        ready([(0, fc), (1, fa), (1, fb)])
+        columns_in(1, third, [sibling])
+        ready([(1, fc)])
+    else:
+        for sub in range(1, subs):
+            planes_in(sub)
+        for sub in range(subs):
+            columns_in(sub, first, b_peers + [sibling])
+        for sub in range(subs):
+            columns_in(sub, second + third, [sibling])
+        ready([(sub, ctx) for sub in range(subs)])
+        for a, b in first + second + third:
+            ready([(sub, column(a, b)) for sub in range(subs)])
 
     for i in range(blocks):
         total = jnp.sum(totals[i], axis=1, keepdims=True)
@@ -293,10 +324,8 @@
             pout_ref[...] = out
         else:
             dout_ref[pl.ds((i - 1) * block, block), :] = out
-    for copy in sent:
+    for copy in sent[len(early) :]:
         copy.wait_send()
-    for copy in sent_inner:
-        pl.when(inner)(copy.wait_send)
 
 
 def body(ctx_count, ep_count, latent, prefill_query, lengths, group_of, own, decode_query):
@@ -308,8 +337,8 @@
     zs = ep_count // 2
     n2 = 2 if ctx_count % 2 == 0 else 1
     n1 = ctx_count // n2
-    halves, packed = layout(rows)
-    copies = 2 * zs + zs * ((n2 - 1) + n2 * (n1 - 1) + ctx_count)
+    subs, halves, packed = layout(rows)
+    copies = subs * zs * (n2 + n2 * (n1 - 1) + ctx_count)
     smem = pl.BlockSpec(memory_space=pltpu.SMEM)
     anywhere = pl.BlockSpec(memory_space=pl.ANY)
     vmem = pl.BlockSpec(memory_space=pltpu.VMEM)
@@ -320,21 +349,23 @@
             jax.ShapeDtypeStruct((p_rows, LAT), jnp.bfloat16),
             jax.ShapeDtypeStruct((d_rows, LAT), jnp.bfloat16),
         ),
-        in_specs=[smem, smem, vmem, anywhere, anywhere, vmem],
+        in_specs=[smem, smem] + [anywhere] * 4,
         out_specs=(vmem, vmem),
         scratch_shapes=[
-            pltpu.VMEM((ctx_count, ep_count, packed, 128), jnp.bfloat16),
+            pltpu.VMEM((subs, ctx_count, ep_count, packed, 128), jnp.bfloat16),
+            pltpu.VMEM((rows, width), jnp.bfloat16),
+            pltpu.VMEM((steps * count, width), jnp.bfloat16),
             pltpu.VMEM((q_count, heads, width), jnp.bfloat16),
             pltpu.VMEM((steps * count, heads, width), jnp.bfloat16),
             pltpu.VMEM((all_rows, LAT), jnp.bfloat16),
             pltpu.VMEM((halves, all_rows, 128), jnp.bfloat16),
             pltpu.VMEM((all_rows, LAT), jnp.float32),
-            pltpu.SemaphoreType.DMA((2,)),
+            pltpu.SemaphoreType.DMA((4,)),
             pltpu.SemaphoreType.DMA((copies,)),
-            pltpu.SemaphoreType.DMA((ctx_count, ep_count)),
+            pltpu.SemaphoreType.DMA((subs, ctx_count, ep_count)),
         ],
         compiler_params=pltpu.CompilerParams(
-            collective_id=0, has_side_effects=True, vmem_limit_bytes=48 * 1024 * 1024
+            collective_id=0, has_side_effects=True, vmem_limit_bytes=60 * 1024 * 1024
         ),
         cost_estimate=pl.CostEstimate(
             flops=2 * pairs * (width + LAT), bytes_accessed=4 << 20, transcendentals=pairs

time: 36.2 us -> 32.3 us (0.89)
  local copies, waits for them, and re-layouts: 6.2 us -> 2.7 us
    unnamed x12 -> x2, local copies, waits for them, and re-layouts: 4.52 us -> 0.01 us
    reshape x1, local copies, waits for them, and re-layouts: 0.77 us -> 1.78 us  [body(): prefill.reshape(q_count, heads, LAT)]
where the time goes in v3:
time: 32.3 us; the launch traced here: 32 us
  Pallas kernels  28.6 us (89%)
  local copies, waits for them, and re-layouts  2.7 us (8%)
  between operations  0.65 us (2%)
    pallas_call x1, Pallas kernels, body(): pl.pallas_call(functools.partial(kernel, (ctx_count, ep_count, heads, ste...  28.6 us
    reshape x1, local copies, waits for them, and re-layouts, body(): prefill.reshape(q_count, heads, LAT)  1.78 us
    reshape x1, local copies, waits for them, and re-layouts, body(): decode.reshape(1, steps, count, heads, LAT)  0.92 us

profile of v3, /device:TPU:0, one launch (start us, length us, event | category | flops | bytes accessed | tf_op | source)
XLA Modules:
  0.0 32.0 jit_solution(10365852122752890841)
XLA Ops:
  0.6 28.6 %shard_map.77 = (bf16[256,512]{1,0:T(8,128)(2,1)}, bf16[512,512]{1,0:T(8,128)(2,1)}) custom-call(s32[2]{0:T(128)} %lengths_ref.1, s32[4]{0:T(128)} %group_ref.1, bf16[64,576]{1,0:T(8,128)(2,1)} %latent_ref.1, bf16[64,4,576]{2,1,0:T(4,128)(2,1)} %pq_ref.1, bf16[128,4,576]{2,1,0:T(4,128)(2,1)} %bitcast.2, bf16[128,576]{1,0:T(8,128)(2,1)} %bitcast.3), custom_call_target="tpu_custom_call" | custom-call | flops 3636461568 | bytes 4194304 | tf_op jit(solution)/shard_map/pallas_call | solution.py:346
  29.3 0.0 copy-start
  29.3 1.8 %reshape.18 = bf16[64,4,512]{2,1,0:T(4,128)(2,1)} reshape(bf16[256,512]{1,0:T(8,128)(2,1)} %get-tuple-element.4) | data formatting | bytes 524288 | tf_op jit(solution)/shard_map/reshape | solution.py:382
  31.0 0.0 copy-done
  31.1 0.9 %reshape.19 = bf16[1,2,64,4,512]{4,3,2,1,0:T(4,128)(2,1)} reshape(bf16[512,512]{1,0:T(8,128)(2,1)S(1)} %copy-done) | data formatting | bytes 1048576 | tf_op jit(solution)/shard_map/reshape | solution.py:383
Async XLA Ops:
  29.3 1.8 %copy-start = (bf16[512,512]{1,0:T(8,128)(2,1)S(1)}, bf16[512,512]{1,0:T(8,128)(2,1)}, u32[]{:S(2)}) copy-start(bf16[512,512]{1,0:T(8,128)(2,1)} %get-tuple-element.5) | copy-start | bytes 1572868

commit v4 on v3

--- a/solution.py
+++ b/solution.py
@@ -318,8 +318,8 @@
             ready([(sub, column(a, b)) for sub in range(subs)])
 
     for i in range(blocks):
-        total = jnp.sum(totals[i], axis=1, keepdims=True)
-        out = (acc[pl.ds(i * block, block), :] / total).astype(jnp.bfloat16)
+        share = 1.0 / jnp.sum(totals[i], axis=1, keepdims=True)
+        out = (acc[pl.ds(i * block, block), :] * share).astype(jnp.bfloat16)
         if i == 0:
             pout_ref[...] = out
         else:

time: 32.3 us -> 32.3 us (level)
  no operation moved by 1% of the time
where the time goes in v4:
time: 32.3 us; the launch traced here: 32 us
  Pallas kernels  28.6 us (89%)
  local copies, waits for them, and re-layouts  2.7 us (8%)
  between operations  0.65 us (2%)
    pallas_call x1, Pallas kernels, body(): pl.pallas_call(functools.partial(kernel, (ctx_count, ep_count, heads, ste...  28.6 us
    reshape x1, local copies, waits for them, and re-layouts, body(): prefill.reshape(q_count, heads, LAT)  1.78 us
    reshape x1, local copies, waits for them, and re-layouts, body(): decode.reshape(1, steps, count, heads, LAT)  0.92 us

profile of v4, /device:TPU:0, one launch (start us, length us, event | category | flops | bytes accessed | tf_op | source)
XLA Modules:
  0.0 32.0 jit_solution(10365852122752890841)
XLA Ops:
  0.6 28.6 %shard_map.77 = (bf16[256,512]{1,0:T(8,128)(2,1)}, bf16[512,512]{1,0:T(8,128)(2,1)}) custom-call(s32[2]{0:T(128)} %lengths_ref.1, s32[4]{0:T(128)} %group_ref.1, bf16[64,576]{1,0:T(8,128)(2,1)} %latent_ref.1, bf16[64,4,576]{2,1,0:T(4,128)(2,1)} %pq_ref.1, bf16[128,4,576]{2,1,0:T(4,128)(2,1)} %bitcast.2, bf16[128,576]{1,0:T(8,128)(2,1)} %bitcast.3), custom_call_target="tpu_custom_call" | custom-call | flops 3636461568 | bytes 4194304 | tf_op jit(solution)/shard_map/pallas_call | solution.py:346
  29.3 0.0 copy-start
  29.3 1.8 %reshape.18 = bf16[64,4,512]{2,1,0:T(4,128)(2,1)} reshape(bf16[256,512]{1,0:T(8,128)(2,1)} %get-tuple-element.4) | data formatting | bytes 524288 | tf_op jit(solution)/shard_map/reshape | solution.py:382
  31.0 0.0 copy-done
  31.1 0.9 %reshape.19 = bf16[1,2,64,4,512]{4,3,2,1,0:T(4,128)(2,1)} reshape(bf16[512,512]{1,0:T(8,128)(2,1)S(1)} %copy-done) | data formatting | bytes 1048576 | tf_op jit(solution)/shard_map/reshape | solution.py:383
Async XLA Ops:
  29.3 1.8 %copy-start = (bf16[512,512]{1,0:T(8,128)(2,1)S(1)}, bf16[512,512]{1,0:T(8,128)(2,1)}, u32[]{:S(2)}) copy-start(bf16[512,512]{1,0:T(8,128)(2,1)} %get-tuple-element.5) | copy-start | bytes 1572868
